TPU v7x, 256 devices: a whole 4x4x8 slice. The times are simulated.
256 devices in a mesh: sta: 128 (over y_lo, x, z, core), win: 2 (over y_hi).
Axes of the slice: x: 4, y: 4 (y_hi: 2, y_lo: 2; y = y_hi * 2 + y_lo), z: 8, core: 2. Of those that a mesh axis runs over, the one named last changes fastest.
Arguments:
- raw_traces: bfloat16 [2, 32768, 4096], P('win', 'sta'), may hold values from -6 to 6
- fir_taps: bfloat16 [127], replicated, may hold values from -0.5 to 0.5
- source_slot: int32 [16, 2048], P('win', 'sta'), may hold values from 0 to 255, as said below
- present: int32 [16, 2048], P('win', 'sta'), may hold values 0 or 1
- lag_start: int32 [2048, 2048], P('sta'), may hold values from -2048 to 1920
Outputs:
- correlations: float32 [2048, 2048, 128], P('sta', 'win')
Inputs may be any that keep to these rules, and one draw needn't show every extreme that they name: `source_slot`: for each win index and each block of 16 stations on one sta index, the 128 entries are distinct; entry e names row e % 2 of the 2 rows that the file device with sta index e // 2 holds for this block. For every block, some file device holds 2 of its traces.
All inputs are finite; a program needn't handle non-finite values. No bound on the sum of `present` on one device may be relied on, other than what follows from the above.
Results may differ from a plain program's by a relative error of at most 0.0093.
Values may be sent and summed in bfloat16 or wider, within the bound.
No kernel may reach another device: no remote copies, remote signals or barrier semaphores. Data moves between devices by JAX's collectives and lax.ppermute only.
A program may use at most 128 MiB of HBM per device.

v0:
```python
import math
import jax
import jax.numpy as jnp
from jax import lax
from jax.sharding import PartitionSpec as P

L = 4096
TAPS = 127
FB = 64
BIN0 = 16
LAGW = 128
tile_len = 128
smooth_half = 4
floor_share = 0.25
spread_eps = 1e-06


def fir_matrix(fir_taps):
    half_taps = (TAPS - 1) // 2
    rows_in = jnp.arange(3 * tile_len, dtype=jnp.int32)[:, None]
    cols_out = jnp.arange(tile_len, dtype=jnp.int32)[None, :]
    offset = rows_in // tile_len - 1
    within = rows_in % tile_len
    tap_index = cols_out - within - offset * tile_len + half_taps
    tap_numbers = jnp.arange(TAPS, dtype=jnp.int32)
    matches = tap_index[:, :, None] == tap_numbers[None, None, :]
    picked = jnp.sum(jnp.where(matches, fir_taps.astype(jnp.float32)[None, None, :], 0.0), axis=2)
    return picked.astype(jnp.bfloat16)


def dft_table():
    sample = jnp.arange(L, dtype=jnp.int32)[:, None]
    bins = BIN0 + jnp.arange(FB, dtype=jnp.int32)[None, :]
    angle = (sample * bins % L).astype(jnp.float32) * (2.0 * math.pi / L)
    return jnp.concatenate([jnp.cos(angle), -jnp.sin(angle)], axis=1).astype(jnp.bfloat16)


def pick_rows(table, slot_list):
    selector = (slot_list[:, None] == jnp.arange(table.shape[0], dtype=jnp.int32)[None, :]).astype(
        table.dtype
    )
    return jnp.dot(selector, table, preferred_element_type=jnp.float32).astype(table.dtype)


def whiten(traces, fir_taps):
    row_count = traces.shape[0]
    tiles = L // tile_len
    blocked = traces.reshape(row_count, tiles, tile_len)
    padded = jnp.pad(blocked, ((0, 0), (1, 1), (0, 0)))
    windowed = jnp.concatenate([padded[:, :-2], padded[:, 1:-1], padded[:, 2:]], axis=2)
    filtered = jnp.dot(
        windowed.reshape(row_count * tiles, 3 * tile_len),
        fir_matrix(fir_taps),
        preferred_element_type=jnp.float32,
    )
    filtered = filtered.reshape(row_count, L).astype(jnp.bfloat16)
    spectrum = jnp.dot(filtered, dft_table(), preferred_element_type=jnp.float32)
    real_part = spectrum[:, :FB]
    imag_part = spectrum[:, FB:]
    magnitude = jnp.sqrt(real_part * real_part + imag_part * imag_part)
    padded_mag = jnp.pad(magnitude, ((0, 0), (smooth_half, smooth_half)))
    running = padded_mag[:, 0:FB]
    for shift_by in range(1, 2 * smooth_half + 1):
        running = running + padded_mag[:, shift_by : shift_by + FB]
    bins = jnp.arange(FB, dtype=jnp.int32)
    counts = (
        jnp.minimum(bins + smooth_half, FB - 1) - jnp.maximum(bins - smooth_half, 0) + 1
    ).astype(jnp.float32)
    amplitude = running / counts[None, :]
    spread = jnp.sqrt(jnp.mean(magnitude * magnitude, axis=1, keepdims=True) + spread_eps)
    divisor = jnp.maximum(amplitude, floor_share * spread)
    return jnp.concatenate([real_part / divisor, imag_part / divisor], axis=1).astype(jnp.bfloat16)


def lag_transform(cross_sum, lag_first, scale_factor):
    bins = BIN0 + jnp.arange(FB, dtype=jnp.int32)
    phase_int = lag_first[..., None] * bins % L
    alpha_angle = phase_int.astype(jnp.float32) * (2.0 * math.pi / L)
    cos_alpha = jnp.cos(alpha_angle)
    sin_alpha = jnp.sin(alpha_angle)
    cross_re = cross_sum[..., :FB]
    cross_im = cross_sum[..., FB:]
    rotated = jnp.concatenate(
        [cross_re * cos_alpha - cross_im * sin_alpha, cross_re * sin_alpha + cross_im * cos_alpha],
        axis=-1,
    )
    lag_index = jnp.arange(LAGW, dtype=jnp.int32)
    beta_angle = (bins[:, None] * lag_index[None, :] % L).astype(jnp.float32) * (2.0 * math.pi / L)
    lag_table = jnp.concatenate([jnp.cos(beta_angle), -jnp.sin(beta_angle)], axis=0)
    flat_rows = rotated.reshape(-1, 2 * FB)
    lag_values = jnp.dot(
        flat_rows, lag_table, precision=lax.Precision.HIGHEST, preferred_element_type=jnp.float32
    )
    return (lag_values * scale_factor).reshape(cross_sum.shape[0], cross_sum.shape[1], LAGW)


def make_accumulate(block_spectra, piece_rows):
    owned = block_spectra.shape[1]
    own_rows = jnp.concatenate([block_spectra[..., :FB], block_spectra[..., FB:]], axis=1)
    row_count = piece_rows.shape[1]
    other_rows = jnp.concatenate([piece_rows[..., :FB], piece_rows[..., FB:]], axis=1)
    product = jnp.einsum("wif,wjf->ijf", own_rows, other_rows, preferred_element_type=jnp.float32)
    real_part = product[:owned, :row_count] + product[owned:, row_count:]
    imag_part = product[owned:, :row_count] - product[:owned, row_count:]
    block_sum = jnp.concatenate([real_part, imag_part], axis=2)
    return block_sum


def per_device(raw_traces, fir_taps, source_slot, present, lag_start):
    local_raw = raw_traces[0]
    win_size = lax.axis_size("win")
    windows_here, owned = source_slot.shape
    flat_slots = source_slot.reshape(-1)
    keep_mask = present.reshape(-1, 1).astype(jnp.bfloat16)
    received = lax.all_to_all(local_raw, "sta", split_axis=0, concat_axis=0, tiled=True)
    traces = pick_rows(received, flat_slots)
    spectra = whiten(traces, fir_taps)
    spectra = (spectra * keep_mask).reshape(windows_here, owned, 2 * FB)
    scale_factor = 1.0 / math.sqrt(FB * windows_here * win_size)
    cross_sum = make_accumulate(spectra, lax.all_gather(spectra, "sta", axis=1, tiled=True))
    lag_values = lag_transform(cross_sum, lag_start, scale_factor)
    correlations = lax.psum_scatter(lag_values, "win", scatter_dimension=1, tiled=True)
    return correlations


def solution(mesh):
    placed = (P("win", "sta", None), P(), P("win", "sta"), P("win", "sta"), P("sta", None))
    return jax.shard_map(
        per_device, mesh=mesh, in_specs=placed, out_specs=P("sta", "win", None), check_vma=False
    )
```

profile of v0, /device:TPU:1, one launch (start us, length us, event | category | flops | bytes accessed | tf_op | source)
XLA Modules:
  0.0 626.0 jit_solution(1351621436093601959)
XLA Ops:
  6.5 4.4 all_to_all.8
  11.0 14.8 %all-to-all-start = ((bf16[128,2,4096]{2,1,0:T(2,128)(2,1)}), bf16[128,2,4096]{2,1,0:T(2,128)(2,1)S(1)}, u32[]{:S(2)}, u32[]{:S(2)}) async-start(bf16[128,2,4096]{2,1,0:T(2,128)(2,1)} %all_to_all.8), calls=%async_computation | async-start | bytes 4194304 | tf_op jit(solution)/shard_map/all_to_all | solution.py:115
  26.0 0.2 subtract_add_fusion
  26.1 2.5 select_reduce_fusion
  28.7 4.9 cosine_convert_fusion
  33.6 43.0 %all-to-all-done = bf16[128,2,4096]{2,1,0:T(2,128)(2,1)S(1)} async-done(((bf16[128,2,4096]{2,1,0:T(2,128)(2,1)}), bf16[128,2,4096]{2,1,0:T(2,128)(2,1)S(1)}, u32[]{:S(2)}, u32[]{:S(2)}) %all-to-all-start) | async-done | bytes 2097184 | tf_op jit(solution)/shard_map/all_to_all | solution.py:115
  76.6 2.2 all_to_all.10
  78.8 2.1 convolution_convert_fusion.1
  80.9 0.5 concatenate.36
  81.4 0.2 copy.30
  81.6 1.0 pad_slice_fusion.1
  82.7 1.0 convolution_convert_fusion
  83.7 0.5 convert_element_type.55
  84.2 0.4 fusion.16
  84.7 0.1 divide_convert_fusion.1
  84.8 0.1 copy.23
  84.9 0.1 copy.22
  85.1 0.1 pad_maximum_fusion.1
  85.2 0.2 copy.24
  85.4 0.8 copy.25
  86.2 0.2 reduce-scatter.2.cloned.1.call-start
  86.4 0.2 fusion.47
  86.7 212.8 %all-gather.2.cloned.1.call-done = bf16[8,2048,128]{2,0,1:T(8,128)(2,1)} async-done(((bf16[8,16,128]{2,0,1:T(8,128)(2,1)}), bf16[8,2048,128]{2,0,1:T(8,128)(2,1)}) %all-gather.2.cloned.1.call-update) | async-done | bytes 4194320 | tf_op jit(solution)/shard_map/all_gather | solution.py:120
  299.5 7.3 %fusion.65 = (bf16[8,2048,64]{2,0,1:T(8,128)(2,1)}, bf16[8,2048,64]{2,0,1:T(8,128)(2,1)}) fusion(bf16[8,2048,128]{2,0,1:T(8,128)(2,1)} %all-gather.2.cloned.1.call-done), kind=kLoop, calls=%fused_computation.116 | loop fusion | bytes 8388608 | tf_op jit(solution)/shard_map/slice | solution.py:101
  306.8 5.8 copy.28
  312.6 6.8 %copy.29 = bf16[8,2048,64]{1,0,2:T(8,128)(2,1)} copy(bf16[8,2048,64]{2,0,1:T(8,128)(2,1)} %get-tuple-element.12) | data formatting | bytes 4194304
  319.4 19.5 %convolution_bitcast_fusion = f32[32,4096,64]{1,0,2:T(8,128)} fusion(bf16[8,2048,64]{1,0,2:T(8,128)(2,1)} %copy.29, bf16[8,2048,64]{1,0,2:T(8,128)(2,1)S(1)} %copy.28, bf16[8,16,64]{1,0,2:T(8,128)(2,1)S(1)} %get-tuple-element.16, bf16[8,16,64]{1,0,2:T(8,128)(2,1)S(1)} %get-tuple-element.15), kind=kOutput, calls=%fused_computation.7 | convolution fusion | flops 142671872 | bytes 37781504 | tf_op jit(solution)/shard_map/wif,wjf->ijf/dot_general | solution.py:102
  338.9 38.1 %multiply_subtract_fusion = (f32[16,2048,64]{1,0,2:T(8,128)S(1)}, f32[16,2048,64]{1,0,2:T(8,128)S(1)}) fusion(s32[64]{0:T(128)S(1)} %iota_add_fusion.2, s32[16,2048]{1,0:T(8,128)S(1)} %copy-done, f32[32,4096,64]{1,0,2:T(8,128)} %convolution_bitcast_fusion), kind=kLoop, calls=%fused_computation.16 | loop fusion | flops 46137344 | bytes 50462976 | tf_op jit(solution)/shard_map/sub | solution.py:84
  377.1 2.4 pad_maximum_fusion
  379.4 14.1 %copy.31 = f32[16,8,16,2048]{3,1,2,0:T(8,128)S(1)} copy(f32[16,8,16,2048]{3,2,1,0:T(8,128)S(1)} %bitcast.19) | data formatting | bytes 33554432
  393.6 29.8 %convolution_multiply_fusion = f32[32768,128]{1,0:T(8,128)} fusion(f32[32768,128]{0,1:T(8,128)S(1)} %bitcast.18, f32[64,128]{1,0:T(8,128)S(1)} %get-tuple-element.18, f32[64,128]{1,0:T(8,128)S(1)} %get-tuple-element.17), kind=kOutput, calls=%fused_computation | convolution fusion | flops 6446661632 | bytes 33619968 | tf_op jit(solution)/shard_map/dot_general | solution.py:91
  423.5 195.7 %reduce-scatter.2.cloned.1.call-done = f32[16,1024,128]{2,1,0:T(8,128)} async-done(((f32[16,2048,128]{2,1,0:T(8,128)}), f32[16,1024,128]{2,1,0:T(8,128)}) %reduce-scatter.2.cloned.1.call-update) | async-done | bytes 8388624 | tf_op jit(solution)/shard_map/reduce_scatter | solution.py:122
  (22 shorter events, 0.3 us)
Async XLA Ops:
  6.5 19.3 %copy-start.1 = (s32[8,16]{1,0:T(8,128)S(1)}, s32[8,16]{1,0:T(8,128)}, u32[]{:S(2)}) copy-start(s32[8,16]{1,0:T(8,128)} %param.7) | copy-start | bytes 1540
  6.5 19.4 %copy-start.3 = (bf16[127]{0:T(256)(128)(2,1)S(1)}, bf16[127]{0:T(256)(128)(2,1)}, u32[]{:S(2)}) copy-start(bf16[127]{0:T(256)(128)(2,1)} %param.6) | copy-start | bytes 766
  6.5 19.4 %copy-start.2 = (s32[8,16]{1,0:T(8,128)S(1)}, s32[8,16]{1,0:T(8,128)}, u32[]{:S(2)}) copy-start(s32[8,16]{1,0:T(8,128)} %param.8) | copy-start | bytes 1540
  11.0 65.6 %all-to-all-start = ((bf16[128,2,4096]{2,1,0:T(2,128)(2,1)}), bf16[128,2,4096]{2,1,0:T(2,128)(2,1)S(1)}, u32[]{:S(2)}, u32[]{:S(2)}) async-start(bf16[128,2,4096]{2,1,0:T(2,128)(2,1)} %all_to_all.8), calls=%async_computation | async-start | bytes 4194304 | tf_op jit(solution)/shard_map/all_to_all | solution.py:115
  25.7 273.7 %all-gather.2.cloned.1.call-start = ((), (), s32[]{:S(2)}) async-start(), calls=%async_computation.2 | async-start | bytes 4227072 | tf_op jit(solution)/shard_map/all_gather | solution.py:120
  86.2 533.0 %reduce-scatter.2.cloned.1.call-start = ((), (), s32[]{:S(2)}) async-start(), calls=%async_computation.3 | async-start | bytes 25165824 | tf_op jit(solution)/shard_map/reduce_scatter | solution.py:122
  319.4 19.5 %copy-start = (s32[16,2048]{1,0:T(8,128)S(1)}, s32[16,2048]{1,0:T(8,128)}, u32[]{:S(2)}) copy-start(s32[16,2048]{1,0:T(8,128)} %param.9) | copy-start | bytes 393220
Sparse Core Ops, SparseCore 0:
  86.3 213.1 all-gather.1
  423.6 195.5 reduce-scatter.1
where the time goes:
time: 626 us
  waiting for transfers between devices  452 us (72%)
  matrix products  52.8 us (8%)
  other arithmetic  48.6 us (8%)
  local copies, waits for them, and re-layouts  44.3 us (7%)
  starting transfers between devices  15 us (2%)
  between operations  13.6 us (2%)
    all_gather x1, waiting for transfers between devices, per_device(): lax.all_gather(spectra, 'sta', axis=1, tiled=True)  213 us
    reduce_scatter x1, waiting for transfers between devices, per_device(): lax.psum_scatter(lag_values, 'win', scatter_dimension=1, tiled=True)  196 us
    all_to_all x1, waiting for transfers between devices, per_device(): lax.all_to_all(local_raw, 'sta', split_axis=0, concat_axis=0, tiled=True)  43 us
    sub x1, other arithmetic, lag_transform(): cross_re * cos_alpha - cross_im * sin_alpha  38.1 us
    dot_general x1, matrix products, lag_transform(): jnp.dot(flat_rows, lag_table, precision=lax.Precision.HIGHEST, preferred_...  29.8 us
    unnamed x12, local copies, waits for them, and re-layouts  27.1 us
    dot_general x1, matrix products, make_accumulate(): jnp.einsum('wif,wjf->ijf', own_rows, other_rows, preferred_element_type=j...  19.5 us
    all_to_all x1, starting transfers between devices, per_device(): lax.all_to_all(local_raw, 'sta', split_axis=0, concat_axis=0, tiled=True)  14.8 us
  transfers between devices with their start and end apart: 3, of which 3 were waited for; matrix products, arithmetic and copies ran while one was open for 1% of the time, Pallas kernels for 0%

commit v1 on v0

--- a/solution.py
+++ b/solution.py
@@ -117,7 +117,12 @@
     spectra = whiten(traces, fir_taps)
     spectra = (spectra * keep_mask).reshape(windows_here, owned, 2 * FB)
     scale_factor = 1.0 / math.sqrt(FB * windows_here * win_size)
-    cross_sum = make_accumulate(spectra, lax.all_gather(spectra, "sta", axis=1, tiled=True))
+    cross_sum = make_accumulate(
+        spectra,
+        jnp.concatenate(
+            lax.all_to_all(jnp.stack([spectra] * lax.axis_size("sta")), "sta", 0, 0), axis=1
+        ),
+    )
     lag_values = lag_transform(cross_sum, lag_start, scale_factor)
     correlations = lax.psum_scatter(lag_values, "win", scatter_dimension=1, tiled=True)
     return correlations

time: 626 us -> 515 us (0.82)
  waiting for transfers between devices: 452 us -> 332 us
  starting transfers between devices: 15 us -> 23.5 us
    all_gather x1 -> x0, waiting for transfers between devices: 213 us -> none  [per_device(): lax.all_gather(spectra, 'sta', axis=1, tiled=True)]
    all_to_all x0 -> x1, waiting for transfers between devices: none -> 94.8 us  [per_device(): lax.all_to_all(jnp.stack([spectra] * lax.axis_size('sta')), 'sta', 0, 0)]
    all_to_all x0 -> x1, starting transfers between devices: none -> 8.64 us  [per_device(): lax.all_to_all(jnp.stack([spectra] * lax.axis_size('sta')), 'sta', 0, 0)]
  transfers between devices with their start and end apart: 3 -> 3, of which waited for: 3 -> 3; matrix products, arithmetic and copies ran while one was open for 1% -> 2% of each run, Pallas kernels for 0% -> 0%
where the time goes in v1:
time: 515 us
  waiting for transfers between devices  332 us (64%)
  matrix products  52.8 us (10%)
  other arithmetic  48.6 us (9%)
  local copies, waits for them, and re-layouts  44.2 us (9%)
  starting transfers between devices  23.5 us (5%)
  between operations  13.6 us (3%)
    reduce_scatter x1, waiting for transfers between devices, per_device(): lax.psum_scatter(lag_values, 'win', scatter_dimension=1, tiled=True)  194 us
    all_to_all x1, waiting for transfers between devices, per_device(): lax.all_to_all(jnp.stack([spectra] * lax.axis_size('sta')), 'sta', 0, 0)  94.8 us
    all_to_all x1, waiting for transfers between devices, per_device(): lax.all_to_all(local_raw, 'sta', split_axis=0, concat_axis=0, tiled=True)  43.1 us
    sub x1, other arithmetic, lag_transform(): cross_re * cos_alpha - cross_im * sin_alpha  38.1 us
    dot_general x1, matrix products, lag_transform(): jnp.dot(flat_rows, lag_table, precision=lax.Precision.HIGHEST, preferred_...  29.9 us
    unnamed x12, local copies, waits for them, and re-layouts  24.7 us
    dot_general x1, matrix products, make_accumulate(): jnp.einsum('wif,wjf->ijf', own_rows, other_rows, preferred_element_type=j...  19.5 us
    all_to_all x1, starting transfers between devices, per_device(): lax.all_to_all(local_raw, 'sta', split_axis=0, concat_axis=0, tiled=True)  14.8 us
  transfers between devices with their start and end apart: 3, of which 3 were waited for; matrix products, arithmetic and copies ran while one was open for 2% of the time, Pallas kernels for 0%

profile of v1, /device:TPU:1, one launch (start us, length us, event | category | flops | bytes accessed | tf_op | source)
XLA Modules:
  0.0 514.8 jit_solution(2759133106707393358)
XLA Ops:
  6.5 4.4 all_to_all.11
  11.0 14.8 %all-to-all-start = ((bf16[128,2,4096]{2,1,0:T(2,128)(2,1)}), bf16[128,2,4096]{2,1,0:T(2,128)(2,1)S(1)}, u32[]{:S(2)}, u32[]{:S(2)}) async-start(bf16[128,2,4096]{2,1,0:T(2,128)(2,1)} %all_to_all.11), calls=%async_computation | async-start | bytes 4194304 | tf_op jit(solution)/shard_map/all_to_all | solution.py:115
  25.9 0.2 subtract_add_fusion
  26.1 2.5 select_reduce_fusion
  28.6 4.9 cosine_convert_fusion
  33.5 43.1 %all-to-all-done = bf16[128,2,4096]{2,1,0:T(2,128)(2,1)S(1)} async-done(((bf16[128,2,4096]{2,1,0:T(2,128)(2,1)}), bf16[128,2,4096]{2,1,0:T(2,128)(2,1)S(1)}, u32[]{:S(2)}, u32[]{:S(2)}) %all-to-all-start) | async-done | bytes 2097184 | tf_op jit(solution)/shard_map/all_to_all | solution.py:115
  76.6 2.2 all_to_all.13
  78.8 2.1 convolution_convert_fusion.1
  80.9 0.5 concatenate.38
  81.4 0.2 copy.36
  81.6 1.0 pad_slice_fusion.1
  82.7 1.0 convolution_convert_fusion
  83.7 0.5 convert_element_type.57
  84.2 0.4 fusion.16
  84.8 0.1 copy.28
  84.9 0.1 copy.27
  85.2 0.2 copy.29
  85.4 0.2 copy.30
  85.6 3.1 stack.3
  88.6 8.6 %all-to-all-start.1 = ((bf16[128,8,16,128]{3,2,1,0:T(8,128)(2,1)}), bf16[128,8,16,128]{3,2,1,0:T(8,128)(2,1)}, u32[]{:S(2)}, u32[]{:S(2)}) async-start(bf16[128,8,16,128]{3,2,1,0:T(8,128)(2,1)} %stack.3), calls=%async_computation.1 | async-start | bytes 8388608 | tf_op jit(solution)/shard_map/all_to_all | solution.py:123
  97.3 0.2 fusion.47
  97.6 94.8 %all-to-all-done.1 = bf16[128,8,16,128]{3,2,1,0:T(8,128)(2,1)} async-done(((bf16[128,8,16,128]{3,2,1,0:T(8,128)(2,1)}), bf16[128,8,16,128]{3,2,1,0:T(8,128)(2,1)}, u32[]{:S(2)}, u32[]{:S(2)}) %all-to-all-start.1) | async-done | bytes 4194336 | tf_op jit(solution)/shard_map/all_to_all | solution.py:123
  192.4 2.9 copy.31
  195.4 4.1 fusion.65
  199.4 4.7 copy.34
  204.1 5.7 %copy.35 = bf16[8,2048,64]{1,0,2:T(8,128)(2,1)} copy(bf16[8,2048,64]{2,1,0:T(8,128)(2,1)} %get-tuple-element.12) | data formatting | bytes 4194304
  209.8 19.5 %convolution_bitcast_fusion = f32[32,4096,64]{1,0,2:T(8,128)} fusion(bf16[8,2048,64]{1,0,2:T(8,128)(2,1)} %copy.35, bf16[8,2048,64]{1,0,2:T(8,128)(2,1)S(1)} %copy.34, bf16[8,16,64]{1,0,2:T(8,128)(2,1)S(1)} %get-tuple-element.16, bf16[8,16,64]{1,0,2:T(8,128)(2,1)S(1)} %get-tuple-element.15), kind=kOutput, calls=%fused_computation.7 | convolution fusion | flops 142671872 | bytes 37781504 | tf_op jit(solution)/shard_map/wif,wjf->ijf/dot_general | solution.py:102
  229.3 38.1 %multiply_subtract_fusion = (f32[16,2048,64]{1,0,2:T(8,128)S(1)}, f32[16,2048,64]{1,0,2:T(8,128)S(1)}) fusion(s32[64]{0:T(128)S(1)} %iota_add_fusion.2, s32[16,2048]{1,0:T(8,128)S(1)} %copy-done, f32[32,4096,64]{1,0,2:T(8,128)} %convolution_bitcast_fusion), kind=kLoop, calls=%fused_computation.16 | loop fusion | flops 46137344 | bytes 50462976 | tf_op jit(solution)/shard_map/sub | solution.py:84
  267.4 2.4 pad_maximum_fusion
  269.8 14.1 %copy.37 = f32[16,8,16,2048]{3,1,2,0:T(8,128)S(1)} copy(f32[16,8,16,2048]{3,2,1,0:T(8,128)S(1)} %bitcast.22) | data formatting | bytes 33554432
  284.0 29.9 %convolution_multiply_fusion = f32[32768,128]{1,0:T(8,128)} fusion(f32[32768,128]{0,1:T(8,128)S(1)} %bitcast.21, f32[64,128]{1,0:T(8,128)S(1)} %get-tuple-element.18, f32[64,128]{1,0:T(8,128)S(1)} %get-tuple-element.17), kind=kOutput, calls=%fused_computation | convolution fusion | flops 6446661632 | bytes 33619968 | tf_op jit(solution)/shard_map/dot_general | solution.py:91
  313.8 194.1 %reduce-scatter.2.cloned.1.call-done = f32[16,1024,128]{2,1,0:T(8,128)} async-done(((f32[16,2048,128]{2,1,0:T(8,128)}), f32[16,1024,128]{2,1,0:T(8,128)}) %reduce-scatter.2.cloned.1.call-update) | async-done | bytes 8388624 | tf_op jit(solution)/shard_map/reduce_scatter | solution.py:127
  (23 shorter events, 0.5 us)
Async XLA Ops:
  6.5 19.2 %copy-start.1 = (s32[8,16]{1,0:T(8,128)S(1)}, s32[8,16]{1,0:T(8,128)}, u32[]{:S(2)}) copy-start(s32[8,16]{1,0:T(8,128)} %param.7) | copy-start | bytes 1540
  6.5 19.3 %copy-start.3 = (bf16[127]{0:T(256)(128)(2,1)S(1)}, bf16[127]{0:T(256)(128)(2,1)}, u32[]{:S(2)}) copy-start(bf16[127]{0:T(256)(128)(2,1)} %param.6) | copy-start | bytes 766
  6.5 19.3 %copy-start.2 = (s32[8,16]{1,0:T(8,128)S(1)}, s32[8,16]{1,0:T(8,128)}, u32[]{:S(2)}) copy-start(s32[8,16]{1,0:T(8,128)} %param.8) | copy-start | bytes 1540
  11.0 65.6 %all-to-all-start = ((bf16[128,2,4096]{2,1,0:T(2,128)(2,1)}), bf16[128,2,4096]{2,1,0:T(2,128)(2,1)S(1)}, u32[]{:S(2)}, u32[]{:S(2)}) async-start(bf16[128,2,4096]{2,1,0:T(2,128)(2,1)} %all_to_all.11), calls=%async_computation | async-start | bytes 4194304 | tf_op jit(solution)/shard_map/all_to_all | solution.py:115
  88.6 103.8 %all-to-all-start.1 = ((bf16[128,8,16,128]{3,2,1,0:T(8,128)(2,1)}), bf16[128,8,16,128]{3,2,1,0:T(8,128)(2,1)}, u32[]{:S(2)}, u32[]{:S(2)}) async-start(bf16[128,8,16,128]{3,2,1,0:T(8,128)(2,1)} %stack.3), calls=%async_computation.1 | async-start | bytes 8388608 | tf_op jit(solution)/shard_map/all_to_all | solution.py:123
  97.3 410.7 %reduce-scatter.2.cloned.1.call-start = ((), (), s32[]{:S(2)}) async-start(), calls=%async_computation.3 | async-start | bytes 25165824 | tf_op jit(solution)/shard_map/reduce_scatter | solution.py:127
  209.8 19.5 %copy-start = (s32[16,2048]{1,0:T(8,128)S(1)}, s32[16,2048]{1,0:T(8,128)}, u32[]{:S(2)}) copy-start(s32[16,2048]{1,0:T(8,128)} %param.9) | copy-start | bytes 393220
Sparse Core Ops, SparseCore 0:
  313.9 193.9 reduce-scatter.1
